TPU v7x, 512 devices: a whole 4x8x8 slice. The times are simulated.
512 devices in a mesh: leaf: 4 (over x), row: 16 (over z, core), col: 8 (over y).
Axes of the slice: x: 4, y: 8, z: 8, core: 2. Of those that a mesh axis runs over, the one named last changes fastest.
Arguments:
- widths: int32 [15], replicated, may hold values from 1024 to 2048, as said below
- bottom_lists: int32 [8, 32], P('leaf'), may hold values from 0 to 47, as said below
- root_inverse: bfloat16 [2048, 2048], P('row')
- second_panels: bfloat16 [4, 2048, 1024], P('leaf', 'row', 'col'), may hold values from -0.09375 to 0.09375
- second_inverse: bfloat16 [4, 1024, 2048], P('leaf', 'col', 'row')
- third_panels: bfloat16 [4, 2, 2048, 2048], P('leaf', None, 'row', 'col'), may hold values from -0.09375 to 0.09375
- third_inverse: bfloat16 [4, 2048, 2048], P('leaf', 'col', 'row')
- bottom_panels: bfloat16 [8, 4096, 2048], P('leaf', 'row', 'col'), may hold values from -0.09375 to 0.09375
- bottom_inverse: bfloat16 [8, 2048, 2048], P('leaf', 'col', 'row')
Outputs:
- second_off: bfloat16 [4, 2048, 1024], P('leaf', 'row', 'col')
- second_diag: bfloat16 [4, 1024, 2048], P('leaf', 'col', 'row')
- third_off: bfloat16 [4, 2, 2048, 2048], P('leaf', None, 'row', 'col')
- third_diag: bfloat16 [4, 2048, 2048], P('leaf', 'col', 'row')
- bottom_off: bfloat16 [8, 3, 2048, 2048], P('leaf', None, 'row', 'col')
- bottom_diag: bfloat16 [8, 2048, 2048], P('leaf', 'col', 'row')
Inputs may be any that keep to these rules, and one draw needn't show every extreme that they name: `widths`: some supernode has 2048 columns and some 2048/2. `bottom_lists`: row e lists 32 different blocks of 128 rows of its chain (root, then second-level ancestor, then parent, 16 blocks each) in increasing order; block 0 and all blocks of the parent are always listed.
All inputs are finite; a program needn't handle non-finite values.
Results may differ from a plain program's by a relative error of at most 0.015.
Values may be sent and summed in bfloat16 or wider, within the bound.
A program may use at most 64 MiB of HBM per device.

v0:
```python
import jax
import jax.numpy as jnp
from jax import lax
from jax.sharding import PartitionSpec as P

NODES = 15
BOTTOM = 8


def partner(block, axis, apart):
    count = lax.axis_size(axis)
    route = []
    for low in range(count):
        high = low | 1 << apart
        if high != low and high < count:
            route += [(low, high), (high, low)]
    return lax.ppermute(block, axis, route)


def node_width(widths, node_at):
    return jnp.sum(jnp.where(jnp.arange(widths.shape[0]) == node_at, widths, 0))


def chain_fold(flat_chain, tile_width, ancestors, shard_piece):
    piece_rows = shard_piece.shape[1]
    picked = jnp.concatenate(
        [
            lax.dynamic_slice_in_dim(flat_chain, level_at * tile_width, piece_rows, 1)
            for level_at in range(ancestors)
        ],
        axis=1,
    )
    stacked = shard_piece.reshape(ancestors * piece_rows, shard_piece.shape[2])
    return jnp.dot(picked, stacked, preferred_element_type=jnp.float32)


def local(
    widths,
    bottom_lists,
    root_inverse,
    second_panels,
    second_inverse,
    third_panels,
    third_inverse,
    bottom_panels,
    bottom_inverse,
):
    group_at = lax.axis_index("leaf")
    row_at = lax.axis_index("row")
    col_at = lax.axis_index("col")
    rows_dev = root_inverse.shape[0]
    tile_width = root_inverse.shape[1]
    half_cols = second_panels.shape[2]
    own_cols = third_panels.shape[3]
    half_at = group_at % 2
    parent_one = 1 + group_at // 2
    node_two = 3 + group_at
    row_first = row_at * rows_dev
    row_index = row_first + jnp.arange(rows_dev)
    root_width = node_width(widths, 0)
    root_mask = (row_index < root_width)[:, None] & (jnp.arange(tile_width) < root_width)[None, :]
    root_block = jnp.where(root_mask, root_inverse, 0)
    width_one = node_width(widths, parent_one)
    mask_rows_one = row_index < width_one
    first_col = half_at * (tile_width // 2) + col_at * half_cols
    mask_cols_one = first_col + jnp.arange(half_cols) < width_one
    panel_one = jnp.where(mask_cols_one[None, :], second_panels[0], 0)
    flat_piece = lax.all_gather(panel_one, "row", axis=0, tiled=True)
    product_one = jnp.dot(root_block, flat_piece, preferred_element_type=jnp.float32)
    off_one = (-product_one).astype(jnp.bfloat16)
    mine_half = lax.all_gather(off_one, "col", axis=1, tiled=True)
    other_half = partner(mine_half, "leaf", 0)
    off_full = jnp.where(
        half_at == 0,
        jnp.concatenate([mine_half, other_half], 1),
        jnp.concatenate([other_half, mine_half], 1),
    )
    term_one = lax.dot_general(
        panel_one, off_full, (((0,), (0,)), ((), ())), preferred_element_type=jnp.float32
    )
    summed_one = lax.psum_scatter(
        term_one.astype(jnp.bfloat16), "row", scatter_dimension=1, tiled=True
    ).astype(jnp.float32)
    inverse_one = jnp.where(
        mask_cols_one[:, None] & mask_rows_one[None, :], second_inverse[0], 0
    ).astype(jnp.float32)
    diag_one = (inverse_one - summed_one).astype(jnp.bfloat16)
    mine_diag = lax.all_gather(diag_one.T, "col", axis=1, tiled=True)
    other_diag = partner(mine_diag, "leaf", 0)
    diag_full = jnp.where(
        half_at == 0,
        jnp.concatenate([mine_diag, other_diag], 1),
        jnp.concatenate([other_diag, mine_diag], 1),
    )
    second_off = off_one[None]
    second_diag = diag_one[None]
    turned_one = lax.all_to_all(off_full, "row", split_axis=1, concat_axis=0, tiled=True)
    chain_two = jnp.stack(
        [jnp.concatenate([root_block, off_full], 1), jnp.concatenate([turned_one.T, diag_full], 1)],
        0,
    )
    flat_two = chain_two.reshape(2 * rows_dev, 2 * tile_width)
    first_own = col_at * own_cols
    width_two = node_width(widths, node_two)
    mask_cols_two = first_own + jnp.arange(own_cols) < width_two
    panel_two = jnp.where(mask_cols_two[None, None, :], third_panels[0], 0)
    product_two = chain_fold(
        flat_two, tile_width, 2, lax.all_gather(panel_two, "row", axis=1, tiled=True)
    )
    off_two = (-product_two).astype(jnp.bfloat16).reshape(2, rows_dev, own_cols)
    full_two = lax.all_gather(off_two, "col", axis=2, tiled=True)
    term_two = jnp.einsum("kin,kim->nm", panel_two, full_two, preferred_element_type=jnp.float32)
    summed_two = lax.psum_scatter(
        term_two.astype(jnp.bfloat16), "row", scatter_dimension=1, tiled=True
    ).astype(jnp.float32)
    mask_rows_two = row_index < width_two
    inverse_two = jnp.where(
        mask_cols_two[:, None] & mask_rows_two[None, :], third_inverse[0], 0
    ).astype(jnp.float32)
    diag_two = (inverse_two - summed_two).astype(jnp.bfloat16)
    diag_rows_two = lax.all_gather(diag_two.T, "col", axis=1, tiled=True)
    turned_two = lax.all_to_all(full_two, "row", split_axis=2, concat_axis=1, tiled=True)
    lower_two = jnp.transpose(turned_two, (2, 0, 1)).reshape(rows_dev, 2 * tile_width)
    chain_three = jnp.stack(
        [
            jnp.concatenate([chain_two[0], full_two[0]], 1),
            jnp.concatenate([chain_two[1], full_two[1]], 1),
            jnp.concatenate([lower_two, diag_rows_two], 1),
        ],
        0,
    )
    flat_three = chain_three.reshape(3 * rows_dev, 3 * tile_width)
    bottom_dev = bottom_panels.shape[0]
    list_len = bottom_lists.shape[1]
    block_rows = 2 * tile_width // list_len
    node_three = NODES - BOTTOM + bottom_dev * group_at + jnp.arange(bottom_dev)
    width_three = jnp.sum(
        jnp.where(jnp.arange(widths.shape[0])[None, :] == node_three[:, None], widths[None, :], 0),
        1,
    )
    mask_cols_three = (first_own + jnp.arange(own_cols))[None, :] < width_three[:, None]
    panel_three = jnp.where(mask_cols_three[:, None, :], bottom_panels, 0)
    positions = (
        jnp.repeat(bottom_lists, block_rows, axis=1) * block_rows
        + jnp.arange(list_len * block_rows) % block_rows
    )
    own_chain = (jnp.arange(3)[:, None] * tile_width + row_index[None, :]).reshape(-1)
    matches = bottom_lists[:, :, None] == (own_chain // block_rows)[None, None, :]
    member = jnp.any(matches, axis=1)
    lower_all = lax.all_gather(panel_three, "row", axis=1, tiled=True)
    spread = jax.vmap(
        lambda where_to, values_in: jnp.zeros((3 * tile_width, own_cols), jnp.bfloat16)
        .at[where_to]
        .set(values_in)
    )(positions, lower_all)
    product_three = jnp.einsum(
        "ab,ebn->ean", flat_three, spread, preferred_element_type=jnp.float32
    )
    chain_rows = lax.dynamic_slice_in_dim(
        spread.reshape(bottom_dev, 3, tile_width, own_cols), row_first, rows_dev, 2
    )
    off_three = jnp.where(member[:, :, None], -product_three, 0.0).astype(jnp.bfloat16)
    off_three = off_three.reshape(bottom_dev, 3, rows_dev, own_cols)
    full_three = lax.all_gather(off_three, "col", axis=3, tiled=True)
    term_three = jnp.einsum(
        "ekin,ekim->enm", chain_rows, full_three, preferred_element_type=jnp.float32
    )
    summed_three = lax.psum_scatter(
        term_three.astype(jnp.bfloat16), "row", scatter_dimension=2, tiled=True
    ).astype(jnp.float32)
    mask_rows_three = row_index[None, :] < width_three[:, None]
    inverse_three = jnp.where(
        mask_cols_three[:, :, None] & mask_rows_three[:, None, :], bottom_inverse, 0
    ).astype(jnp.float32)
    diag_three = (inverse_three - summed_three).astype(jnp.bfloat16)
    return (second_off, second_diag, off_two[None], diag_two[None], off_three, diag_three)


def solution(mesh):
    in_specs = (
        P(),
        P("leaf", None),
        P("row", None),
        P("leaf", "row", "col"),
        P("leaf", "col", "row"),
        P("leaf", None, "row", "col"),
        P("leaf", "col", "row"),
        P("leaf", "row", "col"),
        P("leaf", "col", "row"),
    )
    out_specs = (
        P("leaf", "row", "col"),
        P("leaf", "col", "row"),
        P("leaf", None, "row", "col"),
        P("leaf", "col", "row"),
        P("leaf", None, "row", "col"),
        P("leaf", "col", "row"),
    )
    return jax.shard_map(local, mesh=mesh, in_specs=in_specs, out_specs=out_specs, check_vma=False)
```

profile of v0, /device:TPU:6, one launch (start us, length us, event | category | flops | bytes accessed | tf_op | source)
XLA Modules:
  0.0 519.0 jit_solution(5305973732029650270)
XLA Ops:
  10.2 24.6 %all_gather.24 = bf16[2048,128]{0,1:T(8,128)(2,1)S(1)} all-gather(bf16[128,128]{0,1:T(8,128)(2,1)S(1)} %bitcast_select_fusion.1), channel_id=1, replica_groups=mesh['leaf'=4,'row'=16,'col'=8] {'row'}, dimensions={0}, use_global_device_ids=true | all-gather | bytes 557056 | tf_op jit(solution)/shard_map/all_gather | solution.py:68
  37.7 25.0 %all_gather.25 = bf16[128,1024]{1,0:T(8,128)(2,1)S(1)} all-gather(bf16[128,128]{1,0:T(8,128)(2,1)S(1)} %fusion.7), channel_id=1, replica_groups=mesh['leaf'=4,'row'=16,'col'=8] {'col'}, dimensions={1}, use_global_device_ids=true | all-gather | bytes 294912 | tf_op jit(solution)/shard_map/all_gather | solution.py:71
  62.7 2.9 collective-permute-start
  65.6 5.5 %collective-permute-done = bf16[128,1024]{1,0:T(8,128)(2,1)S(1)} collective-permute-done((bf16[128,1024]{1,0:T(8,128)(2,1)S(1)}, bf16[128,1024]{1,0:T(8,128)(2,1)S(1)}, u32[]{:S(2)}, u32[]{:S(2)}) %collective-permute-start) | collective-permute-done | bytes 262176 | tf_op jit(solution)/shard_map/ppermute | solution.py:17
  74.8 3.6 all-to-all-start
  79.3 48.9 %reduce-scatter.6.cloned.1.call-done = bf16[128,128]{0,1:T(8,128)(2,1)} async-done(((bf16[128,2048]{0,1:T(8,128)(2,1)}), bf16[128,128]{0,1:T(8,128)(2,1)}) %reduce-scatter.6.cloned.1.call-update) | async-done | bytes 32784 | tf_op jit(solution)/shard_map/reduce_scatter | solution.py:81
  129.0 23.9 %all_gather.26 = bf16[128,1024]{1,0:T(8,128)(2,1)S(1)} all-gather(bf16[128,128]{1,0:T(8,128)(2,1)S(1)} %get-tuple-element.37), channel_id=1, replica_groups=mesh['leaf'=4,'row'=16,'col'=8] {'col'}, dimensions={1}, use_global_device_ids=true | all-gather | bytes 294912 | tf_op jit(solution)/shard_map/all_gather | solution.py:88
  156.1 5.2 collective-permute-done.1
  164.0 8.8 %all-gather.5.cloned.1.call-done = bf16[2,2048,256]{2,1,0:T(8,128)(2,1)} async-done(((bf16[2,128,256]{2,1,0:T(8,128)(2,1)}), bf16[2,2048,256]{2,1,0:T(8,128)(2,1)}) %all-gather.5.cloned.1.call-update) | async-done | bytes 2097168 | tf_op jit(solution)/shard_map/all_gather | solution.py:108
  172.8 3.6 fusion.6
  176.5 39.9 %all-gather.7.cloned.1.call-done = bf16[2,128,2048]{2,1,0:T(8,128)(2,1)} async-done(((bf16[2,128,256]{2,1,0:T(8,128)(2,1)}), bf16[2,128,2048]{2,1,0:T(8,128)(2,1)}) %all-gather.7.cloned.1.call-update) | async-done | bytes 1048592 | tf_op jit(solution)/shard_map/all_gather | solution.py:111
  222.9 7.5 %all-to-all-start.1 = ((bf16[2,128,2048]{1,0,2:T(2,128)(2,1)}), bf16[2,128,2048]{1,0,2:T(2,128)(2,1)}, u32[]{:S(2)}, u32[]{:S(2)}) async-start(bf16[2,128,2048]{1,0,2:T(2,128)(2,1)} %copy.69), calls=%async_computation.3 | async-start | bytes 2097152 | tf_op jit(solution)/shard_map/all_to_all | solution.py:122
  233.9 25.0 %all-to-all-done.1 = bf16[2,128,2048]{1,0,2:T(2,128)(2,1)} async-done(((bf16[2,128,2048]{1,0,2:T(2,128)(2,1)}), bf16[2,128,2048]{1,0,2:T(2,128)(2,1)}, u32[]{:S(2)}, u32[]{:S(2)}) %all-to-all-start.1) | async-done | bytes 1048608 | tf_op jit(solution)/shard_map/all_to_all | solution.py:122
  261.2 25.3 %reduce-scatter.8.cloned.1.call-done = bf16[256,128]{0,1:T(8,128)(2,1)} async-done(((bf16[256,2048]{0,1:T(8,128)(2,1)}), bf16[256,128]{0,1:T(8,128)(2,1)}) %reduce-scatter.8.cloned.1.call-update) | async-done | bytes 65552 | tf_op jit(solution)/shard_map/reduce_scatter | solution.py:113
  287.4 26.1 %all_gather.30 = bf16[128,2048]{1,0:T(8,128)(2,1)S(1)} all-gather(bf16[128,256]{1,0:T(8,128)(2,1)S(1)} %get-tuple-element.35), channel_id=1, replica_groups=mesh['leaf'=4,'row'=16,'col'=8] {'col'}, dimensions={1}, use_global_device_ids=true | all-gather | bytes 589824 | tf_op jit(solution)/shard_map/all_gather | solution.py:121
  313.7 3.6 pad_maximum_fusion
  317.3 17.8 %all-gather.9.cloned.1.call-done = bf16[2,4096,256]{2,1,0:T(8,128)(2,1)} async-done(((bf16[2,256,256]{2,1,0:T(8,128)(2,1)}), bf16[2,4096,256]{2,1,0:T(8,128)(2,1)}) %all-gather.9.cloned.1.call-update) | async-done | bytes 4194320 | tf_op jit(solution)/shard_map/all_gather | solution.py:150
  335.1 39.1 %scatter_custom_fusion = bf16[12288,256]{1,0:T(8,128)(2,1)} fusion(s32[8192]{0:T(1024)S(1)} %bitcast.140, bf16[8192,256]{1,0:T(8,128)(2,1)} %bitcast.141, bf16[]{:T(256)} %constant.73.clone.1), kind=kCustom, calls=%fused_computation.3 | custom fusion | bytes 6291968
  374.1 7.6 %fusion.5 = bf16[2,384,256]{1,2,0:T(8,128)(2,1)S(1)} fusion(bf16[2,6144,256]{2,1,0:T(8,128)(2,1)} %bitcast.125, bf16[384,6144,1]{1,0,2:T(8,128)(2,1)} %bitcast.127, pred[2,384]{1,0:T(4,128)(4,1)S(1)} %compare_reduce_fusion), kind=kOutput, calls=%fused_computation.15 | convolution fusion | flops 2416508928 | bytes 11404032 | tf_op jit(solution)/shard_map/ab,ebn->ean/dot_general | solution.py:156
  382.8 55.5 %all-gather.11.cloned.1.call-done = bf16[2,3,128,2048]{3,2,1,0:T(8,128)(2,1)} async-done(((bf16[2,3,128,256]{3,2,1,0:T(8,128)(2,1)}), bf16[2,3,128,2048]{3,2,1,0:T(8,128)(2,1)}) %all-gather.11.cloned.1.call-update) | async-done | bytes 3145744 | tf_op jit(solution)/shard_map/all_gather | solution.py:164
  438.3 3.3 bitcast_convert_fusion
  441.6 3.8 copy.83
  445.4 3.4 copy.91
  450.4 59.9 %reduce-scatter.10.cloned.1.call-done = bf16[128,512]{1,0:T(8,128)(2,1)} async-done(((bf16[2048,512]{1,0:T(8,128)(2,1)}), bf16[128,512]{1,0:T(8,128)(2,1)}) %reduce-scatter.10.cloned.1.call-update) | async-done | bytes 131088
  (101 shorter events, 34.6 us)
Async XLA Ops:
  7.2 66.0 %copy-start.5 = (bf16[1,2,128,256]{3,2,1,0:T(8,128)(2,1)S(1)}, bf16[1,2,128,256]{3,2,1,0:T(8,128)(2,1)}, u32[]{:S(2)}) copy-start(bf16[1,2,128,256]{3,2,1,0:T(8,128)(2,1)} %param.14) | copy-start | bytes 393220
  7.2 121.0 %reduce-scatter.6.cloned.1.call-start = ((), (), s32[]{:S(2)}) async-start(), calls=%async_computation.5 | async-start | bytes 557056 | tf_op jit(solution)/shard_map/reduce_scatter | solution.py:81
  37.7 37.1 %copy-start.4 = (bf16[128,128]{1,0:T(8,128)(2,1)}, bf16[128,128]{1,0:T(8,128)(2,1)S(1)}, u32[]{:S(2)}) copy-start(bf16[128,128]{1,0:T(8,128)(2,1)S(1)} %fusion.7) | copy-start | bytes 98308
  62.7 15.8 %copy-start.8 = (bf16[1,128,128]{2,1,0:T(8,128)(2,1)S(1)}, bf16[1,128,128]{2,1,0:T(8,128)(2,1)}, u32[]{:S(2)}) copy-start(bf16[1,128,128]{2,1,0:T(8,128)(2,1)} %param.13) | copy-start | bytes 98308
  62.7 8.4 %collective-permute-start = (bf16[128,1024]{1,0:T(8,128)(2,1)S(1)}, bf16[128,1024]{1,0:T(8,128)(2,1)S(1)}, u32[]{:S(2)}, u32[]{:S(2)}) collective-permute-start(bf16[128,1024]{1,0:T(8,128)(2,1)S(1)} %all_gather.25), channel_id=1, source_target_pairs={{0,128},{128,0},{256,384},{384,256},{1,129},{129,1},{257,385},{385... | collective-permute-start | bytes 786440 | tf_op jit(solution)/shard_map/ppermute | solution.py:17
  72.4 100.4 %all-gather.5.cloned.1.call-start = ((), (), s32[]{:S(2)}) async-start(), calls=%async_computation.6 | async-start | bytes 2228224 | tf_op jit(solution)/shard_map/all_gather | solution.py:108
  74.8 81.0 %all-to-all-start = ((bf16[128,16,128]{2,0,1:T(8,128)(2,1)}), bf16[128,16,128]{2,0,1:T(8,128)(2,1)S(1)}, u32[]{:S(2)}, u32[]{:S(2)}) async-start(bf16[128,16,128]{2,0,1:T(8,128)(2,1)} %maximum_select_fusion.1), calls=%async_computation.1 | async-start | bytes 1048576 | tf_op jit(solution)/shard_map/all_to_all | solution.py:97
  78.4 138.0 %all-gather.7.cloned.1.call-start = ((), (), s32[]{:S(2)}) async-start(), calls=%async_computation.7 | async-start | bytes 1179648 | tf_op jit(solution)/shard_map/all_gather | solution.py:111
  152.9 8.4 %collective-permute-start.1 = (bf16[128,1024]{1,0:T(8,128)(2,1)S(1)}, bf16[128,1024]{1,0:T(8,128)(2,1)}, u32[]{:S(2)}, u32[]{:S(2)}) collective-permute-start(bf16[128,1024]{1,0:T(8,128)(2,1)S(1)} %all_gather.26), channel_id=1, source_target_pairs={{0,128},{128,0},{256,384},{384,256},{1,129},{129,1},{257,385},{385... | collective-permute-start | bytes 786440 | tf_op jit(solution)/shard_map/ppermute | solution.py:17
  162.4 1.6 copy-start.1
  164.0 52.5 %copy-start.2 = (bf16[2,128,256]{2,1,0:T(8,128)(2,1)S(1)}, bf16[2,128,256]{2,1,0:T(8,128)(2,1)}, u32[]{:S(2)}) copy-start(bf16[2,128,256]{2,1,0:T(8,128)(2,1)} %bitcast_select_fusion) | copy-start | bytes 393220
  172.8 46.6 %copy-start.12 = (s32[15]{0:T(128)S(1)}, s32[15]{0:T(128)}, u32[]{:S(2)}) copy-start(s32[15]{0:T(128)} %param.9) | copy-start | bytes 184
  172.8 46.9 %copy-start.3 = (bf16[2,256,256]{2,1,0:T(8,128)(2,1)S(1)}, bf16[2,256,256]{2,1,0:T(8,128)(2,1)}, u32[]{:S(2)}) copy-start(bf16[2,256,256]{2,1,0:T(8,128)(2,1)} %param.16) | copy-start | bytes 786436
  176.4 44.0 %copy-start.9 = (s32[2,32]{1,0:T(2,128)S(1)}, s32[2,32]{1,0:T(2,128)}, u32[]{:S(2)}) copy-start(s32[2,32]{1,0:T(2,128)} %param.10) | copy-start | bytes 772
  176.4 44.2 %copy-start.11 = (s32[2]{0:T(128)S(1)}, s32[2]{0:T(128)}, u32[]{:S(2)}) copy-start(s32[2]{0:T(128)} %constant.94) | copy-start | bytes 28
  176.4 44.3 %copy-start.10 = (s32[2]{0:T(128)S(1)}, s32[2]{0:T(128)}, u32[]{:S(2)}) copy-start(s32[2]{0:T(128)} %constant.97) | copy-start | bytes 28
  176.5 110.0 %reduce-scatter.8.cloned.1.call-start = ((), (), s32[]{:S(2)}) async-start(), calls=%async_computation.8 | async-start | bytes 1114112 | tf_op jit(solution)/shard_map/reduce_scatter | solution.py:113
  216.4 4.4 copy-start
  219.3 11.2 %copy-start.7 = (bf16[1,256,128]{2,1,0:T(8,128)(2,1)S(1)}, bf16[1,256,128]{2,1,0:T(8,128)(2,1)}, u32[]{:S(2)}) copy-start(bf16[1,256,128]{2,1,0:T(8,128)(2,1)} %param.15) | copy-start | bytes 196612
  219.3 115.8 %all-gather.9.cloned.1.call-start = ((), (), s32[]{:S(2)}) async-start(), calls=%async_computation.9 | async-start | bytes 4456448 | tf_op jit(solution)/shard_map/all_gather | solution.py:150
  222.9 36.0 %all-to-all-start.1 = ((bf16[2,128,2048]{1,0,2:T(2,128)(2,1)}), bf16[2,128,2048]{1,0,2:T(2,128)(2,1)}, u32[]{:S(2)}, u32[]{:S(2)}) async-start(bf16[2,128,2048]{1,0,2:T(2,128)(2,1)} %copy.69), calls=%async_computation.3 | async-start | bytes 2097152 | tf_op jit(solution)/shard_map/all_to_all | solution.py:122
  230.4 207.8 %all-gather.11.cloned.1.call-start = ((), (), s32[]{:S(2)}) async-start(), calls=%async_computation.10 | async-start | bytes 3538944 | tf_op jit(solution)/shard_map/all_gather | solution.py:164
  382.7 127.5 %reduce-scatter.10.cloned.1.call-start = ((), (), s32[]{:S(2)}) async-start(), calls=%async_computation.11 | async-start | bytes 2228224
  445.4 65.9 %copy-start.6 = (bf16[2,256,128]{2,1,0:T(8,128)(2,1)S(1)}, bf16[2,256,128]{2,1,0:T(8,128)(2,1)}, u32[]{:S(2)}) copy-start(bf16[2,256,128]{2,1,0:T(8,128)(2,1)} %param.17) | copy-start | bytes 393220
Sparse Core Ops, SparseCore 0:
  72.5 55.5 reduce-scatter.5
  131.1 41.6 all-gather.4
  176.6 39.8 all-gather.6
  219.4 67.0 reduce-scatter.7
  289.0 45.9 all-gather.8
  382.8 55.3 all-gather.10
  448.9 61.2 reduce-scatter.9
where the time goes:
time: 520 us; the launch traced here: 519 us
  waiting for transfers between devices  292 us (56%)
  blocking collectives  99.6 us (19%)
  local copies, waits for them, and re-layouts  55.7 us (11%)
  other arithmetic  21.2 us (4%)
  matrix products  18.9 us (4%)
  starting transfers between devices  17.1 us (3%)
  between operations  14.6 us (3%)
    unnamed x8, waiting for transfers between devices  60 us
    all_gather x1, waiting for transfers between devices, local(): full_three = lax.all_gather(off_three, 'col', axis=3, tiled=True)  55.5 us
    unnamed x39, local copies, waits for them, and re-layouts  50.3 us
    reduce_scatter x1, waiting for transfers between devices, local(): lax.psum_scatter(term_one.astype(jnp.bfloat16), 'row', scatter_dimension=...  48.9 us
    all_gather x1, waiting for transfers between devices, local(): full_two = lax.all_gather(off_two, 'col', axis=2, tiled=True)  39.9 us
    all_gather x1, blocking collectives, local(): diag_rows_two = lax.all_gather(diag_two.T, 'col', axis=1, tiled=True)  26.1 us
    reduce_scatter x1, waiting for transfers between devices, local(): lax.psum_scatter(term_two.astype(jnp.bfloat16), 'row', scatter_dimension=...  25.3 us
    all_gather x1, blocking collectives, local(): mine_half = lax.all_gather(off_one, 'col', axis=1, tiled=True)  25 us
  transfers between devices with their start and end apart: 11, of which 10 were waited for; matrix products, arithmetic and copies ran while one was open for 4% of the time, Pallas kernels for 0%

commit v1 on v0

v1 whole, which is shorter than its diff:
```python
import jax
import jax.numpy as jnp
from jax import lax
from jax.experimental import pallas as pl
from jax.experimental.pallas import tpu as pltpu
from jax.sharding import PartitionSpec as P

NODES = 15
BOTTOM = 8
F32 = jnp.float32
BF16 = jnp.bfloat16
MESH = pl.DeviceIdType.MESH
SEMS = 320
RING = 8


def dot(a, b):
    return jnp.dot(a, b, preferred_element_type=F32)


def wrap(at):
    return lax.rem(at + 2 * RING, RING)


class Links:
    def __init__(self, send, recv):
        self.send, self.recv = send, recv
        self.used = 0
        self.sent = []

    def take(self, count):
        first = self.used
        self.used += count
        assert self.used <= SEMS
        return first

    def copy(self, src, dst, send_at, recv_at, device):
        return pltpu.make_async_remote_copy(
            src_ref=src,
            dst_ref=dst,
            send_sem=self.send.at[send_at],
            recv_sem=self.recv.at[recv_at],
            device_id=device,
            device_id_type=MESH,
        )

    def start(self, src, dst, send_at, recv_at, device):
        made = self.copy(src, dst, send_at, recv_at, device)
        made.start()
        self.sent.append(made)

    def arrived(self, ref, recv_at, device):
        self.copy(ref, ref, recv_at, recv_at, device).wait_recv()

    def drain(self):
        for made in self.sent:
            made.wait_send()


class Gather:
    def __init__(self, links, slot, me, up, down, heard=None):
        self.links, self.slot, self.me = links, slot, me
        self.up, self.down, self.heard = up, down, heard
        self.base = links.take(16)

    def sem(self, way, step, part):
        return self.base + way * 8 + (step - 1) * 2 + part

    def push(self, owner, way, step, part):
        ref = self.slot(owner, part)
        at = self.sem(way, step, part)
        self.links.start(ref, ref, at, at, self.down if way else self.up)

    def begin(self, part):
        self.push(self.me, 0, 1, part)
        self.push(self.me, 1, 1, part)
        if self.heard is not None:
            self.heard(self.me, part)

    def relay(self, step, part):
        if step == 4:
            ways = (part,)
        else:
            ways = (0, 1)
        for way in ways:
            owner = wrap(self.me + step) if way else wrap(self.me - step)
            self.links.arrived(self.slot(owner, part), self.sem(way, step, part), self.up)
            if step < 3 or (step == 3 and way == part):
                self.push(owner, way, step + 1, part)
            if self.heard is not None:
                self.heard(owner, part)

    def both(self, step):
        self.relay(step, 0)
        self.relay(step, 1)


def kernel(
    widths,
    lists,
    root,
    p1,
    e1,
    p2,
    e2,
    p3,
    e3,
    o1,
    d1,
    o2,
    d2,
    o3,
    d3,
    l1g,
    e1x,
    l2g,
    wg,
    ga,
    gb,
    gc,
    gd,
    ot1,
    ot2,
    acc,
    acc3,
    o3f,
    wt,
    term,
    sib,
    stage,
    landed,
    send,
    recv,
):
    g = lax.axis_index("leaf")
    r = lax.axis_index("row")
    c = lax.axis_index("col")
    z = lax.div(r, 2)
    k = lax.rem(r, 2)
    h = lax.rem(g, 2)
    links = Links(send, recv)
    z_up, z_down = {"row": lax.rem(r + 2, 16)}, {"row": lax.rem(r + 14, 16)}
    y_up, y_down = {"col": wrap(c + 1)}, {"col": wrap(c - 1)}
    other_core = {"row": r + 1 - 2 * k}
    other_leaf = {"leaf": g + 1 - 2 * h}

    barrier = pltpu.get_barrier_semaphore()
    for device in (z_up, z_down, y_up, y_down, other_core, other_leaf):
        pl.semaphore_signal(barrier, inc=1, device_id=device, device_id_type=MESH)
    for source in range(16):
        for column in (lax.rem(r, 8), lax.div(r, 2)):
            pl.semaphore_signal(
                barrier, inc=1, device_id={"row": source, "col": column}, device_id_type=MESH
            )

    w0, w1, w2 = widths[0], widths[1 + lax.div(g, 2)], widths[3 + g]
    lane128 = lax.broadcasted_iota(jnp.int32, (128, 128), 1)
    row128 = lax.broadcasted_iota(jnp.int32, (128, 128), 0)
    lane256 = lax.broadcasted_iota(jnp.int32, (128, 256), 1)
    row_at = r * 128

    l1g[h, r] = jnp.where(h * 1024 + c * 128 + lane128 < w1, p1[0].astype(F32), 0.0).astype(BF16)
    pl.semaphore_wait(barrier, 38)

    x_at = links.take(2)
    links.start(l1g.at[h, r], l1g.at[h, r], x_at, x_at, other_leaf)
    links.start(e1.at[0], e1x.at[h], x_at + 1, x_at + 1, other_leaf)

    def z_gather(slot):
        base = links.take(16)

        def heard(owner, part):
            ref = slot(2 * owner + k, part)
            at = base + owner * 2 + part
            links.start(ref, ref, at, at, other_core)

        def finish():
            for owner in range(RING):
                for part in range(2):
                    links.arrived(slot(2 * owner + 1 - k, part), base + owner * 2 + part, other_core)

        ring = Gather(links, lambda owner, part: slot(2 * owner + k, part), z, z_up, z_down, heard)
        return ring, finish

    ring_l1, finish_l1 = z_gather(lambda who, part: l1g.at[1 - h if part else h, who])
    ring_l2, finish_l2 = z_gather(lambda who, part: l2g.at[part * 16 + who])
    ring_w, finish_w = z_gather(
        lambda who, part: wg.at[part, pl.ds(pl.multiple_of(2 * who, 2), 2)]
    )

    ring_l1.begin(0)
    links.arrived(l1g.at[1 - h, r], x_at, other_leaf)
    ring_l1.begin(1)

    def mask_root(b, carry):
        cols = b * 128 + lane128
        keep = (row_at + row128 < w0) & (cols < w0)
        block = root[:, pl.ds(pl.multiple_of(b * 128, 128), 128)].astype(F32)
        ga[b, 0:128] = jnp.where(keep, block, 0.0).astype(BF16)
        return carry

    lax.fori_loop(0, 16, mask_root, 0)
    own256 = c * 256 + lane256
    for part in range(2):
        l2g[part * 16 + r] = jnp.where(own256 < w2, p2[0, part].astype(F32), 0.0).astype(BF16)
    ring_l1.both(1)
    ring_l1.both(2)
    ring_l2.begin(0)
    ring_l2.begin(1)
    ring_l1.both(3)
    ring_l1.both(4)
    for e in range(2):
        w3 = widths[NODES - BOTTOM + 2 * g + e]
        for u in range(2):
            wg[e, 2 * r + u] = jnp.where(
                own256 < w3, p3[e, u * 128 : u * 128 + 128].astype(F32), 0.0
            ).astype(BF16)
    e1x[h] = e1[0]
    finish_l1()

    def product(target, lhs, rhs, count, fresh=True):
        if fresh:
            target[...] = jnp.zeros(target.shape, F32)

        def body(q, carry):
            target[...] += dot(lhs(q), rhs(q))
            return carry

        lax.fori_loop(0, count, body, 0)

    def wide(ref, blocks, rows=None):
        if rows is None:
            return jnp.concatenate([ref[b] for b in blocks], axis=1)
        return jnp.concatenate([ref[b, rows] for b in blocks], axis=1)

    def panel_one(q):
        return jnp.concatenate(
            [l1g[half, pl.ds(4 * q, 4)].reshape(512, 128) for half in range(2)], axis=1
        )

    top = slice(0, 128)
    mid = slice(128, 256)
    four = lambda q: [4 * q + u for u in range(4)]
    product(acc.at[top], lambda q: wide(ga, four(q), top), panel_one, 4)
    off = -acc[top]
    for half in range(2):
        block = off[:, half * 128 : half * 128 + 128]
        ga[16 + 8 * half + c, top] = block.astype(BF16)
        ot1[half] = block.T.astype(BF16)
    o1[0] = ga[16 + 8 * h + c, top]

    def sixteen(start, at):
        return pl.ds(pl.multiple_of(start + 16 * at, 16), 16)

    def turn(source, slot, dest_row):
        sends = links.take(16)
        first = links.take(16)
        for t in range(2):
            row_to = dest_row(t)
            for apart in range(RING):
                y = wrap(c + apart)
                src = source(t, y)
                dst = slot(r, y)
                at = sends + t * RING + apart
                made = links.copy(src, dst, at, first + r, {"row": row_to, "col": y})
                if apart == 0:
                    local = pltpu.make_async_copy(src, dst, links.recv.at[first + r])
                    pl.when(row_to == r)(local.start)
                    pl.when(row_to != r)(made.start)

                    def wait_made(made=made, row_to=row_to):
                        pl.when(row_to != r)(made.wait_send)

                    waits.append(wait_made)
                else:
                    made.start()
                    links.sent.append(made)

        def finish():
            for source_row in range(16):
                links.arrived(slot(source_row, c), first + source_row, y_up)

        return finish

    waits = []
    finish_t1 = turn(
        lambda t, y: ot1.at[t, sixteen(0, y)],
        lambda who, y: ga.at[who, sixteen(128, y)],
        lambda t: 8 * t + c,
    )
    y_gather = lambda slot: Gather(links, slot, c, y_up, y_down)
    ring_o1 = y_gather(lambda who, part: ga.at[16 + 8 * part + who, top])
    ring_t1 = y_gather(lambda who, part: ga.at[pl.ds(8 * part, 8), sixteen(128, who)])
    ring_d1 = y_gather(lambda who, part: ga.at[16 + 8 * part + who, mid])
    ring_o2 = y_gather(lambda who, part: gb.at[who, pl.ds(128 * part, 128)])
    ring_t2 = y_gather(lambda who, part: gc.at[pl.ds(16 * part, 16), sixteen(0, who)])
    ring_d2 = y_gather(lambda who, part: gd.at[who, pl.ds(64 * part, 64)])
    ring_o3 = y_gather(lambda who, part: o3f.at[part, who])

    finish_t1()
    ring_t1.begin(0)
    ring_t1.begin(1)
    ring_o1.begin(0)
    ring_o1.begin(1)
    ring_l2.both(1)
    ring_t1.both(1)
    ring_t1.both(2)
    ring_l2.both(2)
    ring_t1.both(3)
    ring_o1.both(1)
    ring_t1.both(4)

    links.arrived(e1x.at[1 - h], x_at + 1, other_leaf)
    product(acc.at[top], lambda q: wide(ga, four(q), mid), panel_one, 4)
    for half in range(2):
        keep = (half * 1024 + c * 128 + lane128 < w1) & (row_at + row128 < w1)
        given = jnp.where(keep, e1x[half].astype(F32).T, 0.0)
        turned = given - acc[top, half * 128 : half * 128 + 128]
        ga[16 + 8 * half + c, mid] = turned.astype(BF16)
    ring_d1.begin(0)
    ring_d1.begin(1)
    d1[0] = ga[16 + 8 * h + c, mid].astype(F32).T.astype(BF16)
    ring_l2.both(3)
    ring_o1.both(2)
    ring_d1.both(1)
    ring_l2.both(4)
    ring_w.begin(0)
    ring_w.begin(1)
    ring_o1.both(3)
    ring_d1.both(2)
    ring_o1.both(4)
    ring_d1.both(3)
    finish_l2()
    ring_d1.both(4)

    panel_two = lambda q: l2g[pl.ds(4 * q, 4)].reshape(512, 256)
    product(acc, lambda q: wide(ga, four(q)), panel_two, 8)
    for a in range(2):
        rows = slice(128 * a, 128 * a + 128)
        off = -acc[rows]
        gb[c, rows] = off.astype(BF16)
        for t in range(2):
            ot2[t, a] = off[:, t * 128 : t * 128 + 128].T.astype(BF16)
    finish_t2 = turn(
        lambda t, y: ot2.at[t, :, sixteen(0, y)],
        lambda who, y: gc.at[pl.ds(pl.multiple_of(2 * who, 2), 2), sixteen(0, y)],
        lambda t: 2 * c + t,
    )
    for a in range(2):
        o2[0, a] = gb[c, 128 * a : 128 * a + 128]
    ring_w.both(1)
    finish_t2()
    ring_t2.begin(0)
    ring_t2.begin(1)
    ring_o2.begin(0)
    ring_o2.begin(1)
    ring_t2.both(1)
    ring_t2.both(2)
    ring_w.both(2)
    ring_t2.both(3)
    ring_o2.both(1)
    ring_t2.both(4)

    def panel_turned(q):
        return jnp.concatenate(
            [l2g[2 * q], l2g[16 + 2 * q], l2g[2 * q + 1], l2g[17 + 2 * q]], axis=0
        )

    product(acc.at[top], lambda q: wide(gc, four(q)), panel_turned, 8)
    for half in range(2):
        cols = slice(half * 128, half * 128 + 128)
        keep = (c * 256 + half * 128 + lane128 < w2) & (row_at + row128 < w2)
        given = jnp.where(keep, e2[0, cols].astype(F32).T, 0.0)
        turned = (given - acc[top, cols]).astype(BF16)
        gd[c, :, cols] = turned
        d2[0, cols] = turned.astype(F32).T.astype(BF16)
    ring_d2.begin(0)
    ring_d2.begin(1)
    ring_w.both(3)
    ring_o2.both(2)
    ring_d2.both(1)
    ring_w.both(4)
    ring_o2.both(3)
    ring_d2.both(2)
    ring_o2.both(4)
    ring_d2.both(3)
    finish_w()

    low = slice(256, 384)
    for e in range(2):
        panel = lambda q, e=e: wg[e, pl.ds(4 * q, 4)].reshape(512, 256)
        listed = lambda q, e=e: [lists[e, 4 * q + u] for u in range(4)]
        turned = lambda q, e=e: [
            2 * lax.bitwise_and(b, 15) + lax.shift_right_logical(b, 4) for b in listed(q)
        ]
        product(acc3.at[e, 0:256], lambda q: wide(ga, listed(q)), panel, 4)
        product(acc3.at[e, low], lambda q: wide(gc, turned(q)), panel, 4)
    places = []
    for e in range(2):
        row = []
        for a in range(2):
            found, where = jnp.int32(0), jnp.int32(0)
            for i in range(16):
                hit = lists[e, i] == 16 * a + r
                found, where = jnp.where(hit, 1, found), jnp.where(hit, i, where)
            row.append((found, where))
        row.append((jnp.int32(1), 16 + r))
        places.append(row)
        for a in range(3):
            wt[e, :, 128 * a : 128 * a + 128] = wg[e, row[a][1]].astype(F32).T.astype(BF16)
    ring_d2.both(4)
    for e in range(2):
        parent = lambda q, e=e: wg[e, pl.ds(16 + 4 * q, 4)].reshape(512, 256)
        pair = lambda q: [2 * q, 2 * q + 1]
        product(acc3.at[e, 0:256], lambda q: wide(gb, pair(q)), parent, 4, False)
        product(acc3.at[e, low], lambda q: wide(gd, pair(q)), parent, 4, False)
        for a in range(3):
            rows = slice(128 * a, 128 * a + 128)
            keep = places[e][a][0] > 0
            off = jnp.where(keep, -acc3[e, rows], 0.0).astype(BF16)
            o3f[e, c, rows] = off
            o3[e, a] = off
        ring_o3.begin(e)

    base_sib = links.take(16)

    def update(e, who):
        both = dot(wt[e], o3f[e, who])
        for t in range(2):
            term[t, e, who] = both[:, t * 128 : t * 128 + 128].astype(BF16)
        at = base_sib + e * RING + who
        links.start(term.at[1 - k, e, who], sib.at[e, who], at, at, other_core)

    for e in range(2):
        update(e, c)
    for step in range(1, 5):
        for e in range(2):
            ring_o3.relay(step, e)
            update(e, wrap(c - step))
            if step < 4:
                update(e, wrap(c + step))
    for e in range(2):
        for who in range(RING):
            links.arrived(sib.at[e, who], base_sib + e * RING + who, other_core)

    def mine(e, who):
        return term[k, e, who].astype(F32) + sib[e, who].astype(F32)

    base_sum = links.take(16)
    arm = lambda e, way: 4 if way == e else 3
    slot_sum = lambda e, way, step: (e * 2 + way) * 4 + step - 1
    for step in range(1, 5):
        for e in range(2):
            for way in range(2):
                if step > arm(e, way):
                    continue
                apart = arm(e, way) + 1 - step
                value = mine(e, wrap(z - apart) if way else wrap(z + apart))
                at = slot_sum(e, way, step)
                if step > 1:
                    links.arrived(landed.at[at - 1], base_sum + at - 1, z_up)
                    value = value + landed[at - 1].astype(F32)
                stage[at] = value.astype(BF16)
                links.start(
                    stage.at[at],
                    landed.at[at],
                    base_sum + at,
                    base_sum + at,
                    z_down if way else z_up,
                )
    rows256 = lax.broadcasted_iota(jnp.int32, (256, 128), 0)
    cols256 = lax.broadcasted_iota(jnp.int32, (256, 128), 1)
    for e in range(2):
        w3 = widths[NODES - BOTTOM + 2 * g + e]
        total = mine(e, z)
        for way in range(2):
            at = slot_sum(e, way, arm(e, way))
            links.arrived(landed.at[at], base_sum + at, z_up)
            total = total + landed[at].astype(F32)
        keep = (c * 256 + rows256 < w3) & (row_at + cols256 < w3)
        d3[e] = (jnp.where(keep, e3[e].astype(F32), 0.0) - total).astype(BF16)
    links.drain()
    for wait in waits:
        wait()


def local(widths, lists, root, p1, e1, p2, e2, p3, e3):
    vmem = pl.BlockSpec(memory_space=pltpu.VMEM)
    smem = pl.BlockSpec(memory_space=pltpu.SMEM)
    shapes = [(1, 128, 128), (1, 128, 128), (1, 2, 128, 256), (1, 256, 128), (2, 3, 128, 256), (2, 256, 128)]
    scratch = [
        ((2, 16, 128, 128), BF16),
        ((2, 128, 128), BF16),
        ((32, 128, 256), BF16),
        ((2, 32, 128, 256), BF16),
        ((32, 256, 128), BF16),
        ((8, 256, 256), BF16),
        ((32, 128, 128), BF16),
        ((8, 128, 256), BF16),
        ((2, 128, 128), BF16),
        ((2, 2, 128, 128), BF16),
        ((256, 256), F32),
        ((2, 384, 256), F32),
        ((2, 8, 384, 256), BF16),
        ((2, 256, 384), BF16),
        ((2, 2, 8, 256, 128), BF16),
        ((2, 8, 256, 128), BF16),
        ((16, 256, 128), BF16),
        ((16, 256, 128), BF16),
    ]
    return pl.pallas_call(
        kernel,
        out_shape=[jax.ShapeDtypeStruct(shape, BF16) for shape in shapes],
        in_specs=[smem, smem] + [vmem] * 7,
        out_specs=[vmem] * 6,
        scratch_shapes=[pltpu.VMEM(*one) for one in scratch]
        + [pltpu.SemaphoreType.DMA((SEMS,)), pltpu.SemaphoreType.DMA((SEMS,))],
        compiler_params=pltpu.CompilerParams(
            collective_id=0, has_side_effects=True, vmem_limit_bytes=48 * 1024 * 1024
        ),
    )(widths, lists, root, p1, e1, p2, e2, p3, e3)


def solution(mesh):
    in_specs = (
        P(),
        P("leaf", None),
        P("row", None),
        P("leaf", "row", "col"),
        P("leaf", "col", "row"),
        P("leaf", None, "row", "col"),
        P("leaf", "col", "row"),
        P("leaf", "row", "col"),
        P("leaf", "col", "row"),
    )
    out_specs = (
        P("leaf", "row", "col"),
        P("leaf", "col", "row"),
        P("leaf", None, "row", "col"),
        P("leaf", "col", "row"),
        P("leaf", None, "row", "col"),
        P("leaf", "col", "row"),
    )

    def whole(*args):
        return tuple(
            jax.shard_map(
                lambda *own: tuple(local(*own)),
                mesh=mesh,
                in_specs=in_specs,
                out_specs=out_specs,
                check_vma=False,
            )(*args)
        )

    return whole
```

time: 520 us -> 182 us (0.35)
  waiting for transfers between devices: 292 us -> 0 us
  Pallas kernels: 0 us -> 168 us
  blocking collectives: 99.6 us -> 0 us
  local copies, waits for them, and re-layouts: 55.7 us -> 11.4 us
  other arithmetic: 21.2 us -> 0 us
  matrix products: 18.9 us -> 0 us
  starting transfers between devices: 17.1 us -> 0 us
  between operations: 14.6 us -> 0.66 us
    pallas_call x0 -> x1, Pallas kernels: none -> 168 us  [local(): pl.pallas_call(kernel, out_shape=[jax.ShapeDtypeStruct(shape, BF16) for s...]
    all_gather x4 -> x0, waiting for transfers between devices: 122 us -> none  [the longest x1 55.5 us: local(): full_three = lax.all_gather(off_three, 'col', axis=3, tiled=True)]
    all_gather x4 -> x0, blocking collectives: 99.6 us -> none  [the longest x1 26.1 us: local(): diag_rows_two = lax.all_gather(diag_two.T, 'col', axis=1, tiled=True)]
    reduce_scatter x2 -> x0, waiting for transfers between devices: 74.2 us -> none  [the longest x1 48.9 us: local(): lax.psum_scatter(term_one.astype(jnp.bfloat16), 'row', scatter_dimension=...]
    unnamed x8 -> x0, waiting for transfers between devices: 60 us -> none
    unnamed x39 -> x24, local copies, waits for them, and re-layouts: 50.3 us -> 11.4 us
    all_to_all x2 -> x0, waiting for transfers between devices: 25 us -> none  [the longest x1 25 us: local(): lax.all_to_all(full_two, 'row', split_axis=2, concat_axis=1, tiled=True)]
    dot_general x6 -> x0, matrix products: 18.9 us -> none  [the longest x1 7.6 us: local(): jnp.einsum('ab,ebn->ean', flat_three, spread, preferred_element_type=jnp....]
  transfers between devices with their start and end apart: 11 -> 0, of which waited for: 10 -> 0; matrix products, arithmetic and copies ran while one was open for 4% -> 0% of each run, Pallas kernels for 0% -> 0%
where the time goes in v1:
time: 182 us; the launch traced here: 180 us
  Pallas kernels  168 us (92%)
  local copies, waits for them, and re-layouts  11.4 us (6%)
    pallas_call x1, Pallas kernels, local(): pl.pallas_call(kernel, out_shape=[jax.ShapeDtypeStruct(shape, BF16) for s...  168 us
    unnamed x24, local copies, waits for them, and re-layouts  11.4 us

profile of v1, /device:TPU:6, one launch (start us, length us, event | category | flops | bytes accessed | tf_op | source)
XLA Modules:
  0.0 180.4 jit_solution(9844874329155151400)
XLA Ops:
  0.6 0.0 copy-start
  0.6 1.0 copy-done
  1.7 0.0 copy-start.1
  1.7 0.9 copy-done.1
  2.6 0.0 copy-start.2
  2.6 0.9 copy-done.2
  3.5 0.0 copy-start.3
  3.5 0.9 copy-done.3
  4.4 0.0 copy-start.4
  4.4 0.8 copy-done.4
  5.3 0.0 copy-start.5
  5.3 0.8 copy-done.5
  6.0 0.0 copy-start.6
  6.0 0.8 copy-done.6
  6.8 0.0 copy-start.7
  6.8 0.7 copy-done.7
  7.5 0.7 copy-done.8
  8.1 168.3 %shard_map.136 = (bf16[1,128,128]{2,1,0:T(8,128)(2,1)S(1)}, bf16[1,128,128]{2,1,0:T(8,128)(2,1)S(1)}, bf16[1,2,128,256]{3,2,1,0:T(8,128)(2,1)S(1)}, bf16[1,256,1...) custom-call(s32[15]{0:T(128)S(1)} %copy-done.8, ...), custom_call_target="tpu_custom_call" | custom-call | tf_op jit(solution)/shard_map/pallas_call | solution.py:511
  176.5 0.6 copy.21
  177.1 0.6 copy.22
  177.7 0.7 copy.23
  178.4 0.6 copy.24
  179.0 0.7 copy.25
  179.7 0.7 copy.26
  (1 shorter events, 0.0 us)
Async XLA Ops:
  0.6 1.0 copy-start
  1.7 0.9 copy-start.1
  2.6 0.9 copy-start.2
  3.5 0.9 copy-start.3
  4.4 0.8 copy-start.4
  5.3 0.8 copy-start.5
  6.0 0.8 copy-start.6
  6.8 0.7 copy-start.7
  7.5 0.7 copy-start.8

commit v2 on v1

v2 whole, which is shorter than its diff:
```python
import jax
import jax.numpy as jnp
from jax import lax
from jax.experimental import pallas as pl
from jax.experimental.pallas import tpu as pltpu
from jax.sharding import PartitionSpec as P

NODES = 15
BOTTOM = 8
F32 = jnp.float32
BF16 = jnp.bfloat16
MESH = pl.DeviceIdType.MESH
SEMS = 384
VMEM = 63 * 1024 * 1024
RING = 8


def dot(a, b):
    return jnp.dot(a, b, preferred_element_type=F32)


def wrap(at):
    return lax.rem(at + 2 * RING, RING)


class Links:
    def __init__(self, send, recv):
        self.send, self.recv = send, recv
        self.used = 0
        self.sent = []

    def take(self, count):
        first = self.used
        self.used += count
        assert self.used <= SEMS
        return first

    def copy(self, src, dst, send_at, recv_at, device):
        return pltpu.make_async_remote_copy(
            src_ref=src,
            dst_ref=dst,
            send_sem=self.send.at[send_at],
            recv_sem=self.recv.at[recv_at],
            device_id=device,
            device_id_type=MESH,
        )

    def start(self, src, dst, send_at, recv_at, device):
        made = self.copy(src, dst, send_at, recv_at, device)
        made.start()
        self.sent.append(made)

    def arrived(self, ref, recv_at, device):
        self.copy(ref, ref, recv_at, recv_at, device).wait_recv()

    def drain(self):
        for made in self.sent:
            made.wait_send()


class Gather:
    def __init__(self, links, slot, me, up, down, heard=None, split=False):
        self.links, self.slot, self.me = links, slot, me
        self.up, self.down, self.heard, self.split = up, down, heard, split
        self.base = links.take(16)

    def sem(self, way, step, part):
        return self.base + way * 8 + (step - 1) * 2 + (part or 0)

    def push(self, owner, way, step, part):
        ref = self.slot(owner, part)
        at = self.sem(way, step, part)
        self.links.start(ref, ref, at, at, self.down if way else self.up)

    def begin(self, part=None):
        self.push(self.me, 0, 1, part)
        self.push(self.me, 1, 1, part)
        if self.heard is not None:
            self.heard(self.me, part)

    def relay(self, step, part=None):
        if step == 4:
            for way in (0, 1) if part is None else (part,):
                owner = wrap(self.me + 4)
                self.links.arrived(self.slot(owner, way), self.sem(way, 4, way), self.up)
            if self.heard is not None:
                self.heard(wrap(self.me + 4), part)
            return
        for way in (0, 1):
            owner = wrap(self.me + step) if way else wrap(self.me - step)
            self.links.arrived(self.slot(owner, part), self.sem(way, step, part), self.up)
            if step < 3:
                self.push(owner, way, step + 1, part)
            elif part is None or way == part:
                self.push(owner, way, 4, way)
            if self.heard is not None:
                self.heard(owner, part)

    def both(self, step):
        if self.split:
            self.relay(step, 0)
            self.relay(step, 1)
        else:
            self.relay(step)


def kernel(
    widths,
    lists,
    root_in,
    p1_in,
    e1_in,
    p2_in,
    e2_in,
    p3_in,
    e3_in,
    o1,
    d1,
    o2,
    d2,
    o3,
    d3,
    l1g,
    e1x,
    l2g,
    wg,
    ga,
    gb,
    gc,
    gd,
    ot1,
    ot2,
    acc,
    acc3,
    o3f,
    wt,
    term,
    sib,
    stage,
    landed,
    o3z,
    wtt,
    ot3,
    moved,
    arrived_at,
    root,
    p1,
    e1,
    p2,
    e2,
    p3,
    e3,
    send,
    recv,
    load_sem,
):
    g = lax.axis_index("leaf")
    r = lax.axis_index("row")
    c = lax.axis_index("col")
    z = lax.div(r, 2)
    k = lax.rem(r, 2)
    h = lax.rem(g, 2)
    links = Links(send, recv)
    waits = []
    z_up, z_down = {"row": lax.rem(r + 2, 16)}, {"row": lax.rem(r + 14, 16)}
    y_up, y_down = {"col": wrap(c + 1)}, {"col": wrap(c - 1)}
    other_core = {"row": r + 1 - 2 * k}
    other_leaf = {"leaf": g + 1 - 2 * h}

    barrier = pltpu.get_barrier_semaphore()
    greeted = [z_up, z_down, other_core, other_leaf] + [{"col": wrap(c + d)} for d in range(1, RING)]
    for device in greeted:
        pl.semaphore_signal(barrier, inc=1, device_id=device, device_id_type=MESH)
    loads = {}
    pairs = dict(
        p1=(p1_in, p1), root=(root_in, root), e1=(e1_in, e1), p2=(p2_in, p2),
        p3=(p3_in, p3), e2=(e2_in, e2), e3=(e3_in, e3),
    )
    for at, name in enumerate(pairs):
        loads[name] = pltpu.make_async_copy(*pairs[name], load_sem.at[at])
        loads[name].start()

    w0, w1, w2 = widths[0], widths[1 + lax.div(g, 2)], widths[3 + g]
    lane128 = lax.broadcasted_iota(jnp.int32, (128, 128), 1)
    row128 = lax.broadcasted_iota(jnp.int32, (128, 128), 0)
    lane256 = lax.broadcasted_iota(jnp.int32, (128, 256), 1)
    row_at = r * 128

    loads['p1'].wait()
    l1g[h, r] = jnp.where(h * 1024 + c * 128 + lane128 < w1, p1[0].astype(F32), 0.0).astype(BF16)
    loads['e1'].wait()
    pl.semaphore_wait(barrier, len(greeted))

    x_at = links.take(2)
    links.start(l1g.at[h, r], l1g.at[h, r], x_at, x_at, other_leaf)
    links.start(e1.at[0], e1x.at[h], x_at + 1, x_at + 1, other_leaf)

    def z_gather(slot, split=False):
        base = links.take(16)

        def heard(owner, part):
            ref = slot(2 * owner + k, part)
            at = base + owner * 2 + (part or 0)
            links.start(ref, ref, at, at, other_core)

        def finish():
            for owner in range(RING):
                for part in (0, 1) if split else (None,):
                    at = base + owner * 2 + (part or 0)
                    links.arrived(slot(2 * owner + 1 - k, part), at, other_core)

        mine = lambda owner, part: slot(2 * owner + k, part)
        return Gather(links, mine, z, z_up, z_down, heard, split), finish

    def halves(part, size):
        return pl.ds(0, size) if part is None else pl.ds(part * (size // 2), size // 2)

    def run(start, count):
        return pl.ds(pl.multiple_of(start, count), count)

    ring_l1, finish_l1 = z_gather(lambda who, part: l1g.at[1 - h if part else h, who], True)
    ring_l2, finish_l2 = z_gather(lambda who, part: l2g.at[run(2 * who, 2), halves(part, 128)])
    ring_w, finish_w = z_gather(lambda who, part: wg.at[halves(part, 2), run(2 * who, 2)])
    ring_oz, finish_oz = z_gather(lambda who, part: o3z.at[pl.ds(3 * who, 3), halves(part, 128)])

    ring_l1.begin(0)
    links.arrived(l1g.at[1 - h, r], x_at, other_leaf)
    ring_l1.begin(1)

    def mask_root(b, carry):
        cols = b * 128 + lane128
        keep = (row_at + row128 < w0) & (cols < w0)
        block = root[:, pl.ds(pl.multiple_of(b * 128, 128), 128)].astype(F32)
        ga[b, 0:128] = jnp.where(keep, block, 0.0).astype(BF16)
        return carry

    loads['root'].wait()
    lax.fori_loop(0, 16, mask_root, 0)
    own256 = c * 256 + lane256
    loads['p2'].wait()
    for part in range(2):
        l2g[2 * r + part] = jnp.where(own256 < w2, p2[0, part].astype(F32), 0.0).astype(BF16)
    ring_l1.both(1)
    ring_l1.both(2)
    ring_l2.begin()
    ring_l1.both(3)
    ring_l1.both(4)
    loads['p3'].wait()
    for e in range(2):
        w3 = widths[NODES - BOTTOM + 2 * g + e]
        for u in range(2):
            wg[e, 2 * r + u] = jnp.where(
                own256 < w3, p3[e, u * 128 : u * 128 + 128].astype(F32), 0.0
            ).astype(BF16)
    e1x[h] = e1[0]
    for u in range(2):
        for t in range(2):
            ot3[t, u] = wg[0, 2 * r + u, :, t * 128 : t * 128 + 128].astype(F32).T.astype(BF16)
    finish_l1()

    def product(target, lhs, rhs, count, fresh=True):
        if fresh:
            target[...] = jnp.zeros(target.shape, F32)

        def body(q, carry):
            target[...] += dot(lhs(q), rhs(q))
            return carry

        lax.fori_loop(0, count, body, 0)

    def wide(ref, blocks, rows=None):
        if rows is None:
            return jnp.concatenate([ref[b] for b in blocks], axis=1)
        return jnp.concatenate([ref[b, rows] for b in blocks], axis=1)

    def panel_one(q):
        return jnp.concatenate(
            [l1g[half, pl.ds(4 * q, 4)].reshape(512, 128) for half in range(2)], axis=1
        )

    top = slice(0, 128)
    mid = slice(128, 256)
    four = lambda q: [4 * q + u for u in range(4)]
    product(acc.at[top], lambda q: wide(ga, four(q), top), panel_one, 4)
    off = -acc[top]
    for half in range(2):
        block = off[:, half * 128 : half * 128 + 128]
        ga[16 + 2 * c + half, top] = block.astype(BF16)
        ot1[half] = block.T.astype(BF16)
    o1[0] = ga[16 + 2 * c + h, top]

    def sixteen(start, at):
        return pl.ds(pl.multiple_of(start + 16 * at, 16), 16)

    def turn(source, slot, dest_row):
        sends = links.take(16)
        first = links.take(16)
        for t in range(2):
            row_to = dest_row(t)
            for apart in range(RING):
                y = wrap(c + apart)
                src = source(t, y)
                dst = slot(r, y)
                at = sends + t * RING + apart
                made = links.copy(src, dst, at, first + r, {"row": row_to, "col": y})
                if apart == 0:
                    local = pltpu.make_async_copy(src, dst, links.recv.at[first + r])
                    pl.when(row_to == r)(local.start)
                    pl.when(row_to != r)(made.start)

                    def wait_made(made=made, row_to=row_to):
                        pl.when(row_to != r)(made.wait_send)

                    waits.append(wait_made)
                else:
                    made.start()
                    links.sent.append(made)

        def finish():
            for source_row in range(16):
                links.arrived(slot(source_row, c), first + source_row, y_up)

        return finish

    finish_t1 = turn(
        lambda t, y: ot1.at[t, sixteen(0, y)],
        lambda who, y: ga.at[who, sixteen(128, y)],
        lambda t: 8 * t + c,
    )
    y_gather = lambda slot: Gather(links, slot, c, y_up, y_down)
    ring_o1 = y_gather(
        lambda who, part: ga.at[run(16 + 2 * who, 2) if part is None else 16 + 2 * who + part, top]
    )
    ring_t1 = y_gather(lambda who, part: ga.at[halves(part, 16), sixteen(128, who)])
    ring_d1 = y_gather(
        lambda who, part: ga.at[run(16 + 2 * who, 2) if part is None else 16 + 2 * who + part, mid]
    )
    ring_o2 = y_gather(lambda who, part: gb.at[who, halves(part, 256)])
    ring_t2 = y_gather(lambda who, part: gc.at[halves(part, 32), sixteen(0, who)])
    ring_wt = y_gather(lambda who, part: wtt.at[halves(part, 32), sixteen(0, who)])
    ring_d2 = y_gather(lambda who, part: gd.at[who, halves(part, 128)])
    ring_o3 = y_gather(lambda who, part: o3f.at[who, pl.ds(192 * part, 192) if part is not None else pl.ds(0, 384)])

    finish_t3 = turn(
        lambda t, y: ot3.at[t, :, sixteen(0, y)],
        lambda who, y: wtt.at[run(2 * who, 2), sixteen(0, y)],
        lambda t: 2 * c + t,
    )
    finish_t1()
    ring_t1.begin()
    ring_o1.begin()
    ring_l2.both(1)
    ring_t1.both(1)
    ring_l2.both(2)
    ring_t1.both(2)
    ring_t1.both(3)
    ring_o1.both(1)
    finish_t3()
    ring_wt.begin()
    ring_t1.both(4)

    links.arrived(e1x.at[1 - h], x_at + 1, other_leaf)
    product(acc.at[top], lambda q: wide(ga, four(q), mid), panel_one, 4)
    for half in range(2):
        keep = (half * 1024 + c * 128 + lane128 < w1) & (row_at + row128 < w1)
        given = jnp.where(keep, e1x[half].astype(F32).T, 0.0)
        turned = given - acc[top, half * 128 : half * 128 + 128]
        ga[16 + 2 * c + half, mid] = turned.astype(BF16)
    ring_d1.begin()
    ring_l2.both(3)
    ring_o1.both(2)
    ring_d1.both(1)
    d1[0] = ga[16 + 2 * c + h, mid].astype(F32).T.astype(BF16)
    ring_l2.both(4)
    ring_w.begin()
    ring_o1.both(3)
    ring_d1.both(2)
    ring_wt.both(1)
    ring_d1.both(3)
    ring_o1.both(4)
    finish_l2()
    ring_w.both(1)
    ring_d1.both(4)

    panel_two = lambda q: l2g[pl.ds(4 * q, 4)].reshape(512, 256)
    second = lambda b: 16 + 2 * lax.bitwise_and(b, 7) + lax.shift_right_logical(b, 3)
    crossed = lambda q: [2 * q, second(2 * q), 2 * q + 1, second(2 * q + 1)]
    product(acc, lambda q: wide(ga, crossed(q)), panel_two, 8)
    for a in range(2):
        rows = slice(128 * a, 128 * a + 128)
        off = -acc[rows]
        gb[c, rows] = off.astype(BF16)
        for t in range(2):
            ot2[t, a] = off[:, t * 128 : t * 128 + 128].T.astype(BF16)
    finish_t2 = turn(
        lambda t, y: ot2.at[t, :, sixteen(0, y)],
        lambda who, y: gc.at[pl.ds(pl.multiple_of(2 * who, 2), 2), sixteen(0, y)],
        lambda t: 2 * c + t,
    )
    for a in range(2):
        o2[0, a] = gb[c, 128 * a : 128 * a + 128]
    ring_wt.both(2)
    finish_t2()
    ring_t2.begin()
    ring_o2.begin()
    ring_w.both(2)
    ring_t2.both(1)
    ring_t2.both(2)
    ring_w.both(3)
    ring_t2.both(3)
    ring_o2.both(1)
    ring_t2.both(4)

    loads['e2'].wait()
    product(acc.at[top], lambda q: wide(gc, four(q)), panel_two, 8)
    for half in range(2):
        cols = slice(half * 128, half * 128 + 128)
        keep = (c * 256 + half * 128 + lane128 < w2) & (row_at + row128 < w2)
        given = jnp.where(keep, e2[0, cols].astype(F32).T, 0.0)
        turned = (given - acc[top, cols]).astype(BF16)
        gd[c, :, cols] = turned
        d2[0, cols] = turned.astype(F32).T.astype(BF16)
    ring_d2.begin()
    ring_w.both(4)
    ring_o2.both(2)
    ring_d2.both(1)
    ring_o2.both(3)
    ring_d2.both(2)
    ring_d2.both(3)
    ring_o2.both(4)
    ring_wt.both(3)
    finish_w()

    low = slice(256, 384)
    def placed(b):
        return jnp.where(b < 16, b, second(lax.bitwise_and(b, 15)))

    def paired(b):
        return 2 * lax.bitwise_and(b, 15) + lax.shift_right_logical(b, 4)

    for e in range(2):
        panel = lambda q, e=e: wg[e, pl.ds(4 * q, 4)].reshape(512, 256)
        listed = lambda q, e=e: [lists[e, 4 * q + u] for u in range(4)]
        product(acc3.at[e, 0:256], lambda q: wide(ga, [placed(b) for b in listed(q)]), panel, 4)
        product(acc3.at[e, low], lambda q: wide(gc, [paired(b) for b in listed(q)]), panel, 4)
    places = []
    for e in range(2):
        row = []
        for a in range(2):
            found, where = jnp.int32(0), jnp.int32(0)
            for i in range(16):
                hit = lists[e, i] == 16 * a + r
                found, where = jnp.where(hit, 1, found), jnp.where(hit, i, where)
            row.append((found, where))
        row.append((jnp.int32(1), 16 + r))
        places.append(row)
        for a in range(3):
            if e == 1:
                wt[:, 128 * a : 128 * a + 128] = wg[e, row[a][1]].astype(F32).T.astype(BF16)
    ring_d2.both(4)
    for e in range(2):
        parent = lambda q, e=e: wg[e, pl.ds(16 + 4 * q, 4)].reshape(512, 256)
        pair = lambda q: [2 * q, 2 * q + 1]
        product(acc3.at[e, 0:256], lambda q: wide(gb, pair(q)), parent, 4, False)
        product(acc3.at[e, low], lambda q: wide(gd, pair(q)), parent, 4, False)
        for a in range(3):
            rows = slice(128 * a, 128 * a + 128)
            keep = places[e][a][0] > 0
            off = jnp.where(keep, -acc3[e, rows], 0.0).astype(BF16)
            if e == 0:
                o3z[3 * r + a] = off
            else:
                o3f[c, rows] = off
            o3[e, a] = off
        if e == 0:
            ring_oz.begin()
        else:
            ring_o3.begin()

    base_sib = links.take(8)

    def update(who):
        both = dot(wt[...], o3f[who])
        for t in range(2):
            term[t, who] = both[:, t * 128 : t * 128 + 128].astype(BF16)
        at = base_sib + who
        links.start(term.at[1 - k, who], sib.at[who], at, at, other_core)

    update(c)
    ring_wt.both(4)
    for step in range(1, 5):
        ring_oz.both(step)
        ring_o3.both(step)
        update(wrap(c - step))
        if step < 4:
            update(wrap(c + step))
    for who in range(RING):
        links.arrived(sib.at[who], base_sib + who, other_core)

    def mine(who):
        return term[k, who].astype(F32) + sib[who].astype(F32)

    base_sum = links.take(8)

    def sum_step(step):
        for way in range(2):
            arm = 3 if way else 4
            if step > arm:
                continue
            apart = arm + 1 - step
            value = mine(wrap(z - apart) if way else wrap(z + apart))
            at = way * 4 + step - 1
            if step > 1:
                links.arrived(landed.at[at - 1], base_sum + at - 1, z_up)
                value = value + landed[at - 1].astype(F32)
            stage[at] = value.astype(BF16)
            device = z_down if way else z_up
            links.start(stage.at[at], landed.at[at], base_sum + at, base_sum + at, device)

    sum_step(1)

    finish_oz()
    sum_step(2)
    fold = lambda b: 3 * lax.bitwise_and(b, 15) + lax.shift_right_logical(b, 4)
    product(
        acc.at[top],
        lambda q: wide(wtt, four(q)),
        lambda q: jnp.concatenate([o3z[fold(lists[0, 4 * q + u])] for u in range(4)], axis=0),
        8,
    )
    base_move = links.take(4)
    for t in range(2):
        moved[t] = acc[top, t * 128 : t * 128 + 128].astype(BF16)
    stays = []
    for t in range(2):
        to = {"row": 2 * c + t, "col": z}
        made = links.copy(moved.at[t], arrived_at.at[k], base_move + t, base_move + 2 + k, to)
        own = (2 * c + t == r) & (z == c)
        local = pltpu.make_async_copy(moved.at[t], arrived_at.at[k], links.recv.at[base_move + 2 + k])
        pl.when(own)(local.start)
        pl.when(jnp.logical_not(own))(made.start)
        stays.append((own, made))
    sum_step(3)
    sum_step(4)
    loads['e3'].wait()
    rows256 = lax.broadcasted_iota(jnp.int32, (256, 128), 0)
    cols256 = lax.broadcasted_iota(jnp.int32, (256, 128), 1)

    def given_three(e):
        w3 = widths[NODES - BOTTOM + 2 * g + e]
        keep = (c * 256 + rows256 < w3) & (row_at + cols256 < w3)
        return jnp.where(keep, e3[e].astype(F32), 0.0)

    start = given_three(0)
    for t in range(2):
        links.arrived(arrived_at.at[t], base_move + 2 + t, other_core)
        rows = slice(t * 128, t * 128 + 128)
        d3[0, rows] = (start[rows] - arrived_at[t].astype(F32)).astype(BF16)
    total = mine(z)
    for way in range(2):
        at = 6 if way else 3
        links.arrived(landed.at[at], base_sum + at, z_up)
        total = total + landed[at].astype(F32)
    d3[1] = (given_three(1) - total).astype(BF16)
    links.drain()
    for wait in waits:
        wait()
    for own, made in stays:
        pl.when(jnp.logical_not(own))(made.wait_send)


def write_out(*refs):
    count = len(refs) // 2
    sems = refs[-1]
    copies = [
        pltpu.make_async_copy(refs[i], refs[count + i], sems.at[i]) for i in range(count)
    ]
    for one in copies:
        one.start()
    for one in copies:
        one.wait()


def local(widths, lists, root, p1, e1, p2, e2, p3, e3):
    vmem = pl.BlockSpec(memory_space=pltpu.VMEM)
    smem = pl.BlockSpec(memory_space=pltpu.SMEM)
    shapes = [(1, 128, 128), (1, 128, 128), (1, 2, 128, 256), (1, 256, 128), (2, 3, 128, 256), (2, 256, 128)]
    scratch = [
        ((2, 16, 128, 128), BF16),
        ((2, 128, 128), BF16),
        ((32, 128, 256), BF16),
        ((2, 32, 128, 256), BF16),
        ((32, 256, 128), BF16),
        ((8, 256, 256), BF16),
        ((32, 128, 128), BF16),
        ((8, 128, 256), BF16),
        ((2, 128, 128), BF16),
        ((2, 2, 128, 128), BF16),
        ((256, 256), F32),
        ((2, 384, 256), F32),
        ((8, 384, 256), BF16),
        ((256, 384), BF16),
        ((2, 8, 256, 128), BF16),
        ((8, 256, 128), BF16),
        ((8, 256, 128), BF16),
        ((8, 256, 128), BF16),
        ((48, 128, 256), BF16),
        ((32, 128, 128), BF16),
        ((2, 2, 128, 128), BF16),
        ((2, 128, 128), BF16),
        ((2, 128, 128), BF16),
        ((128, 2048), BF16),
        ((1, 128, 128), BF16),
        ((1, 128, 128), BF16),
        ((1, 2, 128, 256), BF16),
        ((1, 256, 128), BF16),
        ((2, 256, 256), BF16),
        ((2, 256, 128), BF16),
    ]
    hbm = pl.BlockSpec(memory_space=pltpu.HBM)
    made = pl.pallas_call(
        kernel,
        out_shape=[jax.ShapeDtypeStruct(shape, BF16) for shape in shapes],
        in_specs=[smem, smem] + [hbm] * 7,
        out_specs=[vmem] * 6,
        scratch_shapes=[pltpu.VMEM(*one) for one in scratch]
        + [pltpu.SemaphoreType.DMA((count,)) for count in (SEMS, SEMS, 7)],
        compiler_params=pltpu.CompilerParams(
            collective_id=0, has_side_effects=True, vmem_limit_bytes=VMEM
        ),
    )(widths, lists, root, p1, e1, p2, e2, p3, e3)
    return pl.pallas_call(
        write_out,
        out_shape=[jax.ShapeDtypeStruct(shape, BF16) for shape in shapes],
        in_specs=[vmem] * 6,
        out_specs=[hbm] * 6,
        scratch_shapes=[pltpu.SemaphoreType.DMA((6,))],
        compiler_params=pltpu.CompilerParams(vmem_limit_bytes=VMEM),
    )(*made)


def solution(mesh):
    in_specs = (
        P(),
        P("leaf", None),
        P("row", None),
        P("leaf", "row", "col"),
        P("leaf", "col", "row"),
        P("leaf", None, "row", "col"),
        P("leaf", "col", "row"),
        P("leaf", "row", "col"),
        P("leaf", "col", "row"),
    )
    out_specs = (
        P("leaf", "row", "col"),
        P("leaf", "col", "row"),
        P("leaf", None, "row", "col"),
        P("leaf", "col", "row"),
        P("leaf", None, "row", "col"),
        P("leaf", "col", "row"),
    )

    def whole(*args):
        return tuple(
            jax.shard_map(
                lambda *own: tuple(local(*own)),
                mesh=mesh,
                in_specs=in_specs,
                out_specs=out_specs,
                check_vma=False,
            )(*args)
        )

    return whole
```

time: 182 us -> 169 us (0.929)
  local copies, waits for them, and re-layouts: 11.4 us -> 0 us
  Pallas kernels: 168 us -> 166 us
    unnamed x24 -> x0, local copies, waits for them, and re-layouts: 11.4 us -> none
    pallas_call x1, Pallas kernels: 168 us -> 164 us  [local(): pl.pallas_call(kernel, out_shape=[jax.ShapeDtypeStruct(shape, BF16) for s...]
    pallas_call x0 -> x1, Pallas kernels: none -> 2.09 us  [local(): pl.pallas_call(write_out, out_shape=[jax.ShapeDtypeStruct(shape, BF16) fo...]
where the time goes in v2:
time: 169 us; the launch traced here: 167 us
  Pallas kernels  166 us (98%)
    pallas_call x1, Pallas kernels, local(): pl.pallas_call(kernel, out_shape=[jax.ShapeDtypeStruct(shape, BF16) for s...  164 us

profile of v2, /device:TPU:6, one launch (start us, length us, event | category | flops | bytes accessed | tf_op | source)
XLA Modules:
  0.0 166.5 jit_solution(5489833826070368010)
XLA Ops:
  0.6 163.8 %shard_map.136 = (bf16[1,128,128]{2,1,0:T(8,128)(2,1)}, bf16[1,128,128]{2,1,0:T(8,128)(2,1)}, bf16[1,2,128,256]{3,2,1,0:T(8,128)(2,1)}, bf16[1,256,128]{2,1,0:T(...) custom-call(s32[15]{0:T(128)} %widths.1, s32[2,32]{1,0:T(2,128)} %lists.1, ...), custom_call_target="tpu_custom_call" | custom-call | tf_op jit(solution)/shard_map/pallas_call | solution.py:621
  164.5 2.1 %shard_map.137 = (bf16[1,128,128]{2,1,0:T(8,128)(2,1)}, bf16[1,128,128]{2,1,0:T(8,128)(2,1)}, bf16[1,2,128,256]{3,2,1,0:T(8,128)(2,1)}, bf16[1,256,128]{2,1,0:T(...) custom-call(bf16[1,128,128]{2,1,0:T(8,128)(2,1)} %get-tuple-element.12.refs_0_, ...), custom_call_target="tpu_custom_call" | custom-call | tf_op jit(solution)/shard_map/pallas_call | solution.py:632

commit v3 on v2

--- a/solution.py
+++ b/solution.py
@@ -59,49 +59,38 @@
 
 
 class Gather:
-    def __init__(self, links, slot, me, up, down, heard=None, split=False):
+    def __init__(self, links, slot, me, up, down, heard=None):
         self.links, self.slot, self.me = links, slot, me
-        self.up, self.down, self.heard, self.split = up, down, heard, split
+        self.up, self.down, self.heard = up, down, heard
         self.base = links.take(16)
 
     def sem(self, way, step, part):
-        return self.base + way * 8 + (step - 1) * 2 + (part or 0)
+        return self.base + way * 8 + (step - 1) * 2 + part
 
     def push(self, owner, way, step, part):
         ref = self.slot(owner, part)
         at = self.sem(way, step, part)
         self.links.start(ref, ref, at, at, self.down if way else self.up)
 
-    def begin(self, part=None):
-        self.push(self.me, 0, 1, part)
-        self.push(self.me, 1, 1, part)
-        if self.heard is not None:
-            self.heard(self.me, part)
-
-    def relay(self, step, part=None):
-        if step == 4:
-            for way in (0, 1) if part is None else (part,):
-                owner = wrap(self.me + 4)
-                self.links.arrived(self.slot(owner, way), self.sem(way, 4, way), self.up)
+    def begin(self, parts=(0, 1)):
+        for part in parts:
+            self.push(self.me, 0, 1, part)
+            self.push(self.me, 1, 1, part)
             if self.heard is not None:
-                self.heard(wrap(self.me + 4), part)
-            return
-        for way in (0, 1):
+                self.heard(self.me, part)
+
+    def relay(self, step, part):
+        for way in (part,) if step == 4 else (0, 1):
             owner = wrap(self.me + step) if way else wrap(self.me - step)
             self.links.arrived(self.slot(owner, part), self.sem(way, step, part), self.up)
-            if step < 3:
+            if step < 3 or (step == 3 and way == part):
                 self.push(owner, way, step + 1, part)
-            elif part is None or way == part:
-                self.push(owner, way, 4, way)
             if self.heard is not None:
                 self.heard(owner, part)
 
     def both(self, step):
-        if self.split:
-            self.relay(step, 0)
-            self.relay(step, 1)
-        else:
-            self.relay(step)
+        self.relay(step, 0)
+        self.relay(step, 1)
 
 
 def kernel(
@@ -195,37 +184,37 @@
     links.start(l1g.at[h, r], l1g.at[h, r], x_at, x_at, other_leaf)
     links.start(e1.at[0], e1x.at[h], x_at + 1, x_at + 1, other_leaf)
 
-    def z_gather(slot, split=False):
+    def z_gather(slot):
         base = links.take(16)
 
         def heard(owner, part):
             ref = slot(2 * owner + k, part)
-            at = base + owner * 2 + (part or 0)
+            at = base + owner * 2 + part
             links.start(ref, ref, at, at, other_core)
 
         def finish():
             for owner in range(RING):
-                for part in (0, 1) if split else (None,):
-                    at = base + owner * 2 + (part or 0)
+                for part in range(2):
+                    at = base + owner * 2 + part
                     links.arrived(slot(2 * owner + 1 - k, part), at, other_core)
 
         mine = lambda owner, part: slot(2 * owner + k, part)
-        return Gather(links, mine, z, z_up, z_down, heard, split), finish
+        return Gather(links, mine, z, z_up, z_down, heard), finish
 
     def halves(part, size):
-        return pl.ds(0, size) if part is None else pl.ds(part * (size // 2), size // 2)
+        return pl.ds(part * (size // 2), size // 2)
 
     def run(start, count):
         return pl.ds(pl.multiple_of(start, count), count)
 
-    ring_l1, finish_l1 = z_gather(lambda who, part: l1g.at[1 - h if part else h, who], True)
-    ring_l2, finish_l2 = z_gather(lambda who, part: l2g.at[run(2 * who, 2), halves(part, 128)])
-    ring_w, finish_w = z_gather(lambda who, part: wg.at[halves(part, 2), run(2 * who, 2)])
+    ring_l1, finish_l1 = z_gather(lambda who, part: l1g.at[1 - h if part else h, who])
+    ring_l2, finish_l2 = z_gather(lambda who, part: l2g.at[2 * who + part])
+    ring_w, finish_w = z_gather(lambda who, part: wg.at[part, run(2 * who, 2)])
     ring_oz, finish_oz = z_gather(lambda who, part: o3z.at[pl.ds(3 * who, 3), halves(part, 128)])
 
-    ring_l1.begin(0)
+    ring_l1.begin((0,))
     links.arrived(l1g.at[1 - h, r], x_at, other_leaf)
-    ring_l1.begin(1)
+    ring_l1.begin((1,))
 
     def mask_root(b, carry):
         cols = b * 128 + lane128
@@ -329,23 +318,18 @@
     )
     y_gather = lambda slot: Gather(links, slot, c, y_up, y_down)
     ring_o1 = y_gather(
-        lambda who, part: ga.at[run(16 + 2 * who, 2) if part is None else 16 + 2 * who + part, top]
+        lambda who, part: ga.at[16 + 2 * who + part, top]
     )
     ring_t1 = y_gather(lambda who, part: ga.at[halves(part, 16), sixteen(128, who)])
     ring_d1 = y_gather(
-        lambda who, part: ga.at[run(16 + 2 * who, 2) if part is None else 16 + 2 * who + part, mid]
+        lambda who, part: ga.at[16 + 2 * who + part, mid]
     )
     ring_o2 = y_gather(lambda who, part: gb.at[who, halves(part, 256)])
     ring_t2 = y_gather(lambda who, part: gc.at[halves(part, 32), sixteen(0, who)])
     ring_wt = y_gather(lambda who, part: wtt.at[halves(part, 32), sixteen(0, who)])
     ring_d2 = y_gather(lambda who, part: gd.at[who, halves(part, 128)])
-    ring_o3 = y_gather(lambda who, part: o3f.at[who, pl.ds(192 * part, 192) if part is not None else pl.ds(0, 384)])
-
-    finish_t3 = turn(
-        lambda t, y: ot3.at[t, :, sixteen(0, y)],
-        lambda who, y: wtt.at[run(2 * who, 2), sixteen(0, y)],
-        lambda t: 2 * c + t,
-    )
+    ring_o3 = y_gather(lambda who, part: o3f.at[who, halves(part, 384)])
+
     finish_t1()
     ring_t1.begin()
     ring_o1.begin()
@@ -355,8 +339,6 @@
     ring_t1.both(2)
     ring_t1.both(3)
     ring_o1.both(1)
-    finish_t3()
-    ring_wt.begin()
     ring_t1.both(4)
 
     links.arrived(e1x.at[1 - h], x_at + 1, other_leaf)
@@ -367,6 +349,11 @@
         turned = given - acc[top, half * 128 : half * 128 + 128]
         ga[16 + 2 * c + half, mid] = turned.astype(BF16)
     ring_d1.begin()
+    finish_t3 = turn(
+        lambda t, y: ot3.at[t, :, sixteen(0, y)],
+        lambda who, y: wtt.at[run(2 * who, 2), sixteen(0, y)],
+        lambda t: 2 * c + t,
+    )
     ring_l2.both(3)
     ring_o1.both(2)
     ring_d1.both(1)
@@ -375,12 +362,12 @@
     ring_w.begin()
     ring_o1.both(3)
     ring_d1.both(2)
-    ring_wt.both(1)
     ring_d1.both(3)
     ring_o1.both(4)
+    ring_d1.both(4)
     finish_l2()
-    ring_w.both(1)
-    ring_d1.both(4)
+    finish_t3()
+    ring_wt.begin()
 
     panel_two = lambda q: l2g[pl.ds(4 * q, 4)].reshape(512, 256)
     second = lambda b: 16 + 2 * lax.bitwise_and(b, 7) + lax.shift_right_logical(b, 3)
@@ -399,7 +386,8 @@
     )
     for a in range(2):
         o2[0, a] = gb[c, 128 * a : 128 * a + 128]
-    ring_wt.both(2)
+    ring_w.both(1)
+    ring_wt.both(1)
     finish_t2()
     ring_t2.begin()
     ring_o2.begin()
@@ -422,6 +410,7 @@
         d2[0, cols] = turned.astype(F32).T.astype(BF16)
     ring_d2.begin()
     ring_w.both(4)
+    ring_wt.both(2)
     ring_o2.both(2)
     ring_d2.both(1)
     ring_o2.both(3)

time: 169 us -> 168 us (level)
  the two profiles are of different devices: /device:TPU:6 before, /device:TPU:52 now
where the time goes in v3:
time: 168 us
  Pallas kernels  168 us (100%)
    pallas_call x1, Pallas kernels, local(): pl.pallas_call(kernel, out_shape=[jax.ShapeDtypeStruct(shape, BF16) for s...  165 us

profile of v3, /device:TPU:52, one launch (start us, length us, event | category | flops | bytes accessed | tf_op | source)
XLA Modules:
  0.0 168.2 jit_solution(12078557517028502096)
XLA Ops:
  0.6 165.4 %shard_map.136 = (bf16[1,128,128]{2,1,0:T(8,128)(2,1)}, bf16[1,128,128]{2,1,0:T(8,128)(2,1)}, bf16[1,2,128,256]{3,2,1,0:T(8,128)(2,1)}, bf16[1,256,128]{2,1,0:T(...) custom-call(s32[15]{0:T(128)} %widths.1, s32[2,32]{1,0:T(2,128)} %lists.1, ...), custom_call_target="tpu_custom_call" | custom-call | tf_op jit(solution)/shard_map/pallas_call | solution.py:610
  166.1 2.1 %shard_map.137 = (bf16[1,128,128]{2,1,0:T(8,128)(2,1)}, bf16[1,128,128]{2,1,0:T(8,128)(2,1)}, bf16[1,2,128,256]{3,2,1,0:T(8,128)(2,1)}, bf16[1,256,128]{2,1,0:T(...) custom-call(bf16[1,128,128]{2,1,0:T(8,128)(2,1)} %get-tuple-element.12.refs_0_, ...), custom_call_target="tpu_custom_call" | custom-call | tf_op jit(solution)/shard_map/pallas_call | solution.py:621

commit v4 on v3

--- a/solution.py
+++ b/solution.py
@@ -335,11 +335,14 @@
     ring_o1.begin()
     ring_l2.both(1)
     ring_t1.both(1)
+    ring_o1.both(1)
     ring_l2.both(2)
     ring_t1.both(2)
+    ring_o1.both(2)
     ring_t1.both(3)
-    ring_o1.both(1)
+    ring_o1.both(3)
     ring_t1.both(4)
+    ring_o1.both(4)
 
     links.arrived(e1x.at[1 - h], x_at + 1, other_leaf)
     product(acc.at[top], lambda q: wide(ga, four(q), mid), panel_one, 4)
@@ -355,15 +358,12 @@
         lambda t: 2 * c + t,
     )
     ring_l2.both(3)
-    ring_o1.both(2)
     ring_d1.both(1)
     d1[0] = ga[16 + 2 * c + h, mid].astype(F32).T.astype(BF16)
     ring_l2.both(4)
     ring_w.begin()
-    ring_o1.both(3)
     ring_d1.both(2)
     ring_d1.both(3)
-    ring_o1.both(4)
     ring_d1.both(4)
     finish_l2()
     finish_t3()
@@ -393,11 +393,14 @@
     ring_o2.begin()
     ring_w.both(2)
     ring_t2.both(1)
+    ring_o2.both(1)
     ring_t2.both(2)
+    ring_o2.both(2)
     ring_w.both(3)
     ring_t2.both(3)
-    ring_o2.both(1)
+    ring_o2.both(3)
     ring_t2.both(4)
+    ring_o2.both(4)
 
     loads['e2'].wait()
     product(acc.at[top], lambda q: wide(gc, four(q)), panel_two, 8)
@@ -409,14 +412,11 @@
         gd[c, :, cols] = turned
         d2[0, cols] = turned.astype(F32).T.astype(BF16)
     ring_d2.begin()
+    ring_d2.both(1)
     ring_w.both(4)
+    ring_d2.both(2)
     ring_wt.both(2)
-    ring_o2.both(2)
-    ring_d2.both(1)
-    ring_o2.both(3)
-    ring_d2.both(2)
     ring_d2.both(3)
-    ring_o2.both(4)
     ring_wt.both(3)
     finish_w()
 
@@ -427,11 +427,17 @@
     def paired(b):
         return 2 * lax.bitwise_and(b, 15) + lax.shift_right_logical(b, 4)
 
-    for e in range(2):
-        panel = lambda q, e=e: wg[e, pl.ds(4 * q, 4)].reshape(512, 256)
-        listed = lambda q, e=e: [lists[e, 4 * q + u] for u in range(4)]
-        product(acc3.at[e, 0:256], lambda q: wide(ga, [placed(b) for b in listed(q)]), panel, 4)
-        product(acc3.at[e, low], lambda q: wide(gc, [paired(b) for b in listed(q)]), panel, 4)
+    acc3[...] = jnp.zeros(acc3.shape, F32)
+
+    def above(at, carry):
+        e, q = lax.div(at, 4), lax.rem(at, 4)
+        panel = wg[e, pl.ds(4 * q, 4)].reshape(512, 256)
+        listed = [lists[e, 4 * q + u] for u in range(4)]
+        acc3[e, 0:256] += dot(wide(ga, [placed(b) for b in listed]), panel)
+        acc3[e, low] += dot(wide(gc, [paired(b) for b in listed]), panel)
+        return carry
+
+    lax.fori_loop(0, 8, above, 0)
     places = []
     for e in range(2):
         row = []
@@ -447,11 +453,16 @@
             if e == 1:
                 wt[:, 128 * a : 128 * a + 128] = wg[e, row[a][1]].astype(F32).T.astype(BF16)
     ring_d2.both(4)
+
+    def beside(at, carry):
+        e, q = lax.div(at, 4), lax.rem(at, 4)
+        panel = wg[e, pl.ds(16 + 4 * q, 4)].reshape(512, 256)
+        acc3[e, 0:256] += dot(wide(gb, [2 * q, 2 * q + 1]), panel)
+        acc3[e, low] += dot(wide(gd, [2 * q, 2 * q + 1]), panel)
+        return carry
+
     for e in range(2):
-        parent = lambda q, e=e: wg[e, pl.ds(16 + 4 * q, 4)].reshape(512, 256)
-        pair = lambda q: [2 * q, 2 * q + 1]
-        product(acc3.at[e, 0:256], lambda q: wide(gb, pair(q)), parent, 4, False)
-        product(acc3.at[e, low], lambda q: wide(gd, pair(q)), parent, 4, False)
+        lax.fori_loop(4 * e, 4 * e + 4, beside, 0)
         for a in range(3):
             rows = slice(128 * a, 128 * a + 128)
             keep = places[e][a][0] > 0
@@ -468,21 +479,27 @@
 
     base_sib = links.take(8)
 
-    def update(who):
+    def shared(who):
+        return links.copy(
+            term.at[1 - k, who], sib.at[who], base_sib + who, base_sib + who, other_core
+        )
+
+    def update(who, carry):
         both = dot(wt[...], o3f[who])
         for t in range(2):
             term[t, who] = both[:, t * 128 : t * 128 + 128].astype(BF16)
-        at = base_sib + who
-        links.start(term.at[1 - k, who], sib.at[who], at, at, other_core)
-
-    update(c)
+        shared(who).start()
+        return carry
+
+    def passed(who, carry):
+        shared(who).wait_send()
+        return carry
+
     ring_wt.both(4)
     for step in range(1, 5):
         ring_oz.both(step)
         ring_o3.both(step)
-        update(wrap(c - step))
-        if step < 4:
-            update(wrap(c + step))
+    lax.fori_loop(0, RING, update, 0)
     for who in range(RING):
         links.arrived(sib.at[who], base_sib + who, other_core)
 
@@ -552,6 +569,7 @@
         total = total + landed[at].astype(F32)
     d3[1] = (given_three(1) - total).astype(BF16)
     links.drain()
+    lax.fori_loop(0, RING, passed, 0)
     for wait in waits:
         wait()
     for own, made in stays:

time: 168 us -> 172 us (1.024)
  the two profiles are of different devices: /device:TPU:52 before, /device:TPU:54 now
where the time goes in v4:
time: 172 us; the launch traced here: 171 us
  Pallas kernels  171 us (99%)
    pallas_call x1, Pallas kernels, local(): pl.pallas_call(kernel, out_shape=[jax.ShapeDtypeStruct(shape, BF16) for s...  169 us

profile of v4, /device:TPU:54, one launch (start us, length us, event | category | flops | bytes accessed | tf_op | source)
XLA Modules:
  0.0 171.4 jit_solution(12451755242073576728)
XLA Ops:
  0.6 168.6 %shard_map.136 = (bf16[1,128,128]{2,1,0:T(8,128)(2,1)}, bf16[1,128,128]{2,1,0:T(8,128)(2,1)}, bf16[1,2,128,256]{3,2,1,0:T(8,128)(2,1)}, bf16[1,256,128]{2,1,0:T(...) custom-call(s32[15]{0:T(128)} %widths.1, s32[2,32]{1,0:T(2,128)} %lists.1, ...), custom_call_target="tpu_custom_call" | custom-call | tf_op jit(solution)/shard_map/pallas_call | solution.py:628
  169.3 2.1 %shard_map.137 = (bf16[1,128,128]{2,1,0:T(8,128)(2,1)}, bf16[1,128,128]{2,1,0:T(8,128)(2,1)}, bf16[1,2,128,256]{3,2,1,0:T(8,128)(2,1)}, bf16[1,256,128]{2,1,0:T(...) custom-call(bf16[1,128,128]{2,1,0:T(8,128)(2,1)} %get-tuple-element.12.refs_0_, ...), custom_call_target="tpu_custom_call" | custom-call | tf_op jit(solution)/shard_map/pallas_call | solution.py:639
